TPU v7x, 128 devices: a whole 4x4x4 slice. The times are simulated.
128 devices in a mesh: mp: 8 (over z, x_lo), dp: 16 (over x_hi, y, core).
Axes of the slice: x: 4 (x_hi: 2, x_lo: 2; x = x_hi * 2 + x_lo), y: 4, z: 4, core: 2. Of those that a mesh axis runs over, the one named last changes fastest.
Arguments:
- volume: bfloat16 [16, 64, 64, 2048], P('dp', 'mp'), may hold values from -6 to 6
- kernel_a: bfloat16 [3, 3, 3, 32, 64], replicated, may hold values from -0.21875 to 0.21875
- kernel_b: bfloat16 [3, 3, 3, 64, 128], P(None, None, None, 'mp'), may hold values from -0.15625 to 0.15625
- cotangent: bfloat16 [16, 16, 16, 16, 128], P('dp', None, None, None, 'mp'), may hold values from -6 to 6
Outputs:
- features: bfloat16 [16, 16, 16, 16, 128], P('dp', None, None, None, 'mp')
- grad_a: float32 [3, 3, 3, 32, 64], replicated
- grad_b: float32 [3, 3, 3, 64, 128], P(None, None, None, 'mp')
All inputs are finite; a program needn't handle non-finite values.
Results may differ from a plain program's by a relative error of at most 0.0049.
Values may be sent and summed in bfloat16 or wider, within the bound.
A program may use at most 192 MiB of HBM per device.

v0:
```python
import math
import jax
import jax.numpy as jnp
from jax import lax
from jax.sharding import PartitionSpec as P

GRID = 64


def shifted(array, axis, by):
    size = lax.axis_size(axis)
    pairs = [(i, i + by) for i in range(size) if 0 <= i + by < size]
    return lax.ppermute(array, axis, pairs)


def forward_conv(padded, kernel):
    return lax.conv_general_dilated(
        padded,
        kernel,
        (2, 2, 2),
        "VALID",
        dimension_numbers=("NDHWC", "DHWIO", "NDHWC"),
        preferred_element_type=jnp.float32,
    )


def kernel_grad(padded, grads):
    result = lax.conv_general_dilated(
        padded,
        grads,
        (1, 1, 1),
        "VALID",
        rhs_dilation=(2, 2, 2),
        dimension_numbers=("CDHWN", "IDHWO", "NDHWC"),
        preferred_element_type=jnp.float32,
    )
    return jnp.transpose(result, (1, 2, 3, 0, 4))


def input_grad(grads, kernel, first_low):
    flipped = kernel[::-1, ::-1, ::-1]
    return lax.conv_general_dilated(
        grads,
        flipped,
        (1, 1, 1),
        ((first_low, 2), (1, 2), (1, 2)),
        lhs_dilation=(2, 2, 2),
        dimension_numbers=("NDHWC", "DHWOI", "NDHWC"),
        preferred_element_type=jnp.float32,
    )


def pad_sides(field):
    return jnp.pad(field, ((0, 0), (0, 0), (1, 0), (1, 0), (0, 0)))


def pad_low(field):
    return jnp.pad(field, ((0, 0), (1, 0), (1, 0), (1, 0), (0, 0)))


def shards(volume, kernel_a, kernel_b, cotangent):
    samp_local = volume.shape[0]
    planes = volume.shape[1]
    edge = volume.shape[2]
    in_chan = kernel_a.shape[3]
    field = volume.reshape(samp_local, planes, edge, edge, in_chan)
    below = shifted(field[:, planes - 1 :], "mp", 1)
    padded_x = pad_sides(jnp.concatenate([below, field], axis=1))
    pre = forward_conv(padded_x, kernel_a)
    hidden = jnp.where(pre > 0, pre, 0.3 * pre).astype(jnp.bfloat16)
    grouped = lax.all_to_all(hidden, "mp", split_axis=4, concat_axis=1, tiled=True)
    padded_h = pad_low(grouped)
    partial_out = forward_conv(padded_h, kernel_b)
    features = lax.psum_scatter(partial_out, "mp", scatter_dimension=4, tiled=True).astype(
        jnp.bfloat16
    )
    upstream = lax.all_gather(cotangent, "mp", axis=4, tiled=True)
    local_b = kernel_grad(padded_h, upstream)
    back_group = input_grad(upstream, kernel_b, 1).astype(jnp.bfloat16)
    back = lax.all_to_all(back_group, "mp", split_axis=1, concat_axis=4, tiled=True)
    delta = (back.astype(jnp.float32) * jnp.where(pre > 0, 1.0, 0.3)).astype(jnp.bfloat16)
    local_a = kernel_grad(padded_x, delta)
    total_a = lax.psum(local_a, ("mp", "dp"))
    total_b = lax.psum(local_b, "dp")
    samples_all = samp_local * lax.axis_size("dp")
    grad_a = total_a / math.sqrt(samples_all * (GRID // 2) ** 3)
    grad_b = total_b / math.sqrt(samples_all * (GRID // 4) ** 3)
    return (features, grad_a, grad_b)


def solution(mesh):
    return jax.shard_map(
        shards,
        mesh=mesh,
        in_specs=(
            P("dp", "mp", None, None),
            P(),
            P(None, None, None, "mp", None),
            P("dp", None, None, None, "mp"),
        ),
        out_specs=(P("dp", None, None, None, "mp"), P(), P(None, None, None, "mp", None)),
        check_vma=False,
    )
```

profile of v0, /device:TPU:1, one launch (start us, length us, event | category | flops | bytes accessed | tf_op | source)
XLA Modules:
  0.0 838.3 jit_solution(7763710412680146833)
XLA Ops:
  7.2 4.9 copy.124
  12.0 1.1 slice.11
  13.1 1.1 copy.125
  14.2 4.0 collective-permute-start
  18.2 31.5 %copy.127 = bf16[1,8,64,64,32]{4,0,3,2,1:T(2,128)(2,1)} copy(bf16[1,8,64,64,32]{2,4,3,1,0:T(8,128)(2,1)} %bitcast.69) | data formatting | bytes 4194304 | tf_op jit(solution)/shard_map/reshape | solution.py:66
  49.7 2.7 copy.126
  52.4 58.2 %pad_maximum_fusion = bf16[1,9,64,64,32]{4,0,3,2,1:T(2,128)(2,1)} fusion(bf16[1,8,64,64,32]{4,0,3,2,1:T(2,128)(2,1)} %copy.127, bf16[1,1,64,64,32]{4,0,3,2,1:T(2,128)(2,1)S(1)} %copy.126), kind=kLoop, calls=%fused_computation.4 | loop fusion | flops 1179648 | bytes 4718592 | tf_op jit(solution)/shard_map/concatenate | solution.py:68
  110.6 33.5 %copy.128 = bf16[1,9,64,64,32]{3,4,2,1,0:T(8,128)(2,1)} copy(bf16[1,9,64,64,32]{4,0,3,2,1:T(2,128)(2,1)} %pad_maximum_fusion) | data formatting | bytes 4718592 | tf_op jit(solution)/shard_map/concatenate | solution.py:68
  144.1 9.2 %copy.159 = bf16[9,64,1,64,32]{1,4,3,0,2:T(8,128)(2,1)} copy(bf16[9,64,1,64,32]{3,4,2,1,0:T(8,128)(2,1)} %bitcast.72) | data formatting | bytes 4718592
  153.3 6.1 pad.4.clone
  159.4 15.6 %copy.131 = bf16[9,64,1,8,10,32]{5,3,4,1,0,2:T(8,128)(2,1)} copy(bf16[9,64,1,8,10,32]{1,5,4,3,0,2:T(8,128)(2,1)} %bitcast.67) | data formatting | bytes 5898240 | tf_op jit(solution)/shard_map/conv_general_dilated | solution.py:17
  175.1 2.3 slice.12
  177.4 12.0 %compare_select_fusion = (f32[4,32,8,5,64]{4,2,3,1,0:T(8,128)}, bf16[4,32,8,5,64]{4,2,3,1,0:T(8,128)(2,1)S(1)}) fusion(pred[8,5]{0,1:T(8,128)(4,1)S(1)} %copy-done.6, bf16[3,3,3,32,64]{4,3,2,1,0:T(8,128)(2,1)S(1)} %copy-done, bf16[9,64,1,7,2,32]{5,3,4,1,0,2:T(8,128)(2,1)S(1)} %slice.12, bf16[9,64,1,8,10,32]{5,3,4,1,0,2:T(8,128)(2,1)} %copy.131), kind=kOutput, calls=%fused_computation.20 | convolution fusion | flops 572915712 | bytes 5541928 | tf_op jit(solution)/shard_map/conv_general_dilated | solution.py:17
  189.5 0.3 copy.132
  189.7 0.1 slice_bitcast_fusion.2
  189.8 3.2 copy.133
  193.1 2.7 reshape.71
  195.8 6.1 all-to-all-start
  202.0 3.9 copy.140
  205.9 0.5 copy.149
  206.4 0.2 slice.18
  206.6 2.8 copy.158
  209.4 1.5 all-to-all-done
  210.8 1.0 reshape.72
  211.9 2.9 copy.134
  214.8 2.2 copy.135
  216.9 3.4 copy.160
  220.4 4.0 pad.6.clone
  224.4 12.8 %copy.138 = bf16[32,32,1,8,6,8]{5,3,4,1,0,2:T(8,128)(2,1)} copy(bf16[32,32,1,8,6,8]{1,5,4,3,0,2:T(8,128)(2,1)} %bitcast.73) | data formatting | bytes 1572864 | tf_op jit(solution)/shard_map/conv_general_dilated | solution.py:17
  237.2 3.4 slice.14
  240.6 12.3 %broadcast_select_fusion = f32[16,16,8,3,128]{4,2,3,1,0:T(8,128)S(1)} fusion(pred[8,3]{0,1:T(4,128)(4,1)S(1)} %copy-done.7, bf16[3,3,3,8,128]{4,3,2,1,0:T(8,128)(2,1)S(1)} %copy-done.5, bf16[32,32,1,7,2,8]{5,3,4,1,0,2:T(8,128)(2,1)S(1)} %slice.14, bf16[32,32,1,8,6,8]{5,3,4,1,0,2:T(8,128)(2,1)} %copy.138), kind=kOutput, calls=%fused_computation.30 | convolution fusion | flops 329662464 | bytes 4216856 | tf_op jit(solution)/shard_map/conv_general_dilated | solution.py:17
  252.9 2.3 copy.139
  255.2 23.8 %copy.153 = bf16[1,32,32,32,8]{4,0,3,2,1:T(2,128)(2,1)} copy(bf16[1,32,32,32,8]{3,4,2,1,0:T(8,128)(2,1)S(1)} %bitcast.71) | data formatting | bytes 1048576 | tf_op jit(solution)/shard_map/all_to_all | solution.py:71
  279.0 97.7 %all-gather.2.cloned.1.call-done = bf16[1,16,16,16,128]{3,2,1,0,4:T(8,128)(2,1)} async-done(((bf16[1,16,16,16,16]{3,2,1,0,4:T(8,128)(2,1)}), bf16[1,16,16,16,128]{3,2,1,0,4:T(8,128)(2,1)}) %all-gather.2.cloned.1.call-update) | async-done | bytes 1048592 | tf_op jit(solution)/shard_map/all_gather | solution.py:77
  376.7 10.0 %copy.141 = bf16[1,16,16,16,128]{4,3,2,1,0:T(8,128)(2,1)S(1)} copy(bf16[1,16,16,16,128]{3,2,1,0,4:T(8,128)(2,1)} %all-gather.2.cloned.1.call-done) | data formatting | bytes 2097152 | tf_op jit(solution)/shard_map/all_gather | solution.py:77
  386.7 0.3 copy.161
  387.0 0.3 pad.8.clone
  387.4 0.4 copy.144
  387.8 0.2 slice.16
  387.9 14.3 %fusion.17 = bf16[32,32,8,6,8]{4,2,3,1,0:T(8,128)(2,1)} fusion(bf16[3,3,3,8,128]{4,3,2,1,0:T(8,128)(2,1)S(1)} %copy-done.5, bf16[16,16,1,7,1,128]{5,3,4,1,0,2:T(8,128)(2,1)S(1)} %slice.16, bf16[16,16,1,8,3,128]{5,3,4,1,0,2:T(8,128)(2,1)S(1)} %copy.144), kind=kOutput, calls=%fused_computation.24 | convolution fusion | flops 332021760 | bytes 2873344 | tf_op jit(solution)/shard_map/conv_general_dilated | solution.py:42
  402.2 13.6 %copy.145 = bf16[32,32,8,6,8]{1,4,3,2,0:T(8,128)(2,1)S(1)} copy(bf16[32,32,8,6,8]{4,2,3,1,0:T(8,128)(2,1)} %fusion.17) | data formatting | bytes 1572864 | tf_op jit(solution)/shard_map/conv_general_dilated | solution.py:42
  415.8 0.9 select_convert_fusion
  416.7 0.2 fusion.34
  417.0 2.7 reshape.73
  419.7 4.9 all-to-all-start.1
  424.6 13.5 %copy.154 = bf16[1,16,16,16,128]{4,0,3,2,1:T(2,128)(2,1)S(1)} copy(bf16[1,16,16,16,128]{3,2,1,0,4:T(8,128)(2,1)} %all-gather.2.cloned.1.call-done) | data formatting | bytes 2097152 | tf_op jit(solution)/shard_map/all_gather | solution.py:77
  438.1 51.8 %fusion.36 = f32[3,3,3,8,128]{4,3,2,1,0:T(8,128)} fusion(bf16[1,32,32,32,8]{4,0,3,2,1:T(2,128)(2,1)} %copy.153, bf16[1,16,16,16,128]{4,0,3,2,1:T(2,128)(2,1)S(1)} %copy.154), kind=kOutput, calls=%fused_computation.46 | convolution fusion | flops 212629504 | bytes 1683456 | tf_op jit(solution)/shard_map/transpose | solution.py:37
  489.9 0.0 all-reduce.3.cloned.1.call-start
  490.0 1.3 reshape.74
  491.3 3.4 copy.147
  494.7 3.5 fusion.12
  498.2 4.1 copy.151
  502.3 46.6 %fusion.35 = f32[3,3,3,32,64]{4,3,2,1,0:T(8,128)} fusion(bf16[1,9,64,64,32]{4,0,3,2,1:T(2,128)(2,1)} %pad_maximum_fusion, bf16[1,4,32,32,64]{4,0,3,2,1:T(2,128)(2,1)} %copy.151), kind=kOutput, calls=%fused_computation.45 | convolution fusion | flops 443596800 | bytes 3104768 | tf_op jit(solution)/shard_map/transpose | solution.py:37
  548.9 1.6 slice_bitcast_fusion.1
  550.5 14.3 %copy.156 = f32[1,16,16,16,128]{2,3,1,0,4:T(8,128)} copy(f32[1,16,16,16,128]{4,2,3,1,0:T(8,128)} %slice_bitcast_fusion.1) | data formatting | bytes 4194304
  564.8 15.3 %reshape.69 = f32[128,4096]{1,0:T(8,128)} reshape(f32[128,1,16,16,16]{4,3,2,1,0:T(8,128)} %bitcast.66) | data formatting | bytes 4194304
  580.1 45.1 %all-reduce.5.cloned.1.call-done = f32[3,3,3,8,128]{4,3,2,1,0:T(8,128)} async-done(((f32[3,3,3,8,128]{4,3,2,1,0:T(8,128)}), f32[3,3,3,8,128]{4,3,2,1,0:T(8,128)}) %all-reduce.5.cloned.1.call-update) | async-done | bytes 110608 | tf_op jit(solution)/shard_map/psum | solution.py:84
  625.2 1.6 broadcast_multiply_fusion.1
  626.8 147.3 %all-reduce.3.cloned.1.call-done = f32[3,3,3,32,64]{4,3,2,1,0:T(8,128)} async-done(((f32[3,3,3,32,64]{4,3,2,1,0:T(8,128)}), f32[3,3,3,32,64]{4,3,2,1,0:T(8,128)}) %all-reduce.3.cloned.1.call-update) | async-done | bytes 221200 | tf_op jit(solution)/shard_map/psum | solution.py:83
  774.1 1.8 broadcast_multiply_fusion
  775.9 51.3 %reduce-scatter.4.cloned.1.call-done = f32[16,4096]{1,0:T(8,128)} async-done(((f32[128,4096]{1,0:T(8,128)}), f32[16,4096]{1,0:T(8,128)}) %reduce-scatter.4.cloned.1.call-update) | async-done | bytes 262160
  827.2 1.7 reshape.70
  829.0 1.2 copy.157
  830.2 1.2 copy.155
  (25 shorter events, 0.2 us)
Async XLA Ops:
  7.2 170.2 %copy-start = (bf16[3,3,3,32,64]{4,3,2,1,0:T(8,128)(2,1)S(1)}, bf16[3,3,3,32,64]{4,3,2,1,0:T(8,128)(2,1)}, u32[]{:S(2)}) copy-start(bf16[3,3,3,32,64]{4,3,2,1,0:T(8,128)(2,1)} %param.5) | copy-start | bytes 331780
  14.2 35.5 %collective-permute-start = (bf16[1,1,64,64,32]{3,4,2,1,0:T(8,128)(2,1)S(1)}, bf16[1,1,64,64,32]{3,4,2,1,0:T(8,128)(2,1)S(1)}, u32[]{:S(2)}, u32[]{:S(2)}) collective-permute-start(bf16[1,1,64,64,32]{3,4,2,1,0:T(8,128)(2,1)S(1)} %copy.125), channel_id=1, source_target_pairs={{0,16},{16,32},{32,48},{48,64},{64,80},{80,96},{96,112},{1,17},{17... | collective-permute-start | bytes 786440 | tf_op jit(solution)/shard_map/ppermute | solution.py:13
  175.0 2.4 copy-start.6
  195.8 10.1 %copy-start.3 = (f32[4,32,8,5,64]{4,2,3,1,0:T(8,128)S(1)}, f32[4,32,8,5,64]{4,2,3,1,0:T(8,128)}, u32[]{:S(2)}) copy-start(f32[4,32,8,5,64]{4,2,3,1,0:T(8,128)} %get-tuple-element.18) | copy-start | bytes 3932164
  195.8 15.0 %all-to-all-start = ((bf16[8,2,16384]{2,1,0:T(2,128)(2,1)}), bf16[8,2,16384]{2,1,0:T(2,128)(2,1)S(1)}, u32[]{:S(2)}, u32[]{:S(2)}) async-start(bf16[8,2,16384]{2,1,0:T(2,128)(2,1)} %reshape.71), calls=%async_computation | async-start | bytes 1048576 | tf_op jit(solution)/shard_map/all_to_all | solution.py:71
  202.0 174.8 %all-gather.2.cloned.1.call-start = ((), (), s32[]{:S(2)}) async-start(), calls=%async_computation.3 | async-start | bytes 9437184 | tf_op jit(solution)/shard_map/all_gather | solution.py:77
  237.2 3.4 copy-start.5
  237.2 3.5 copy-start.7
  402.2 13.6 %copy-start.4 = (pred[8,6]{1,0:T(8,128)(4,1)S(1)}, pred[8,6]{1,0:T(8,128)(4,1)}, u32[]{:S(2)}) copy-start(pred[8,6]{1,0:T(8,128)(4,1)} %constant.31) | copy-start | bytes 148
  419.7 70.3 %all-to-all-start.1 = ((bf16[8,2,16384]{2,1,0:T(2,128)(2,1)}), bf16[8,2,16384]{2,1,0:T(2,128)(2,1)S(1)}, u32[]{:S(2)}, u32[]{:S(2)}) async-start(bf16[8,2,16384]{2,1,0:T(2,128)(2,1)} %reshape.73), calls=%async_computation.1 | async-start | bytes 1048576 | tf_op jit(solution)/shard_map/all_to_all | solution.py:80
  424.6 200.6 %all-reduce.5.cloned.1.call-start = ((), (), s32[]{:S(2)}) async-start(), calls=%async_computation.5 | async-start | bytes 221184 | tf_op jit(solution)/shard_map/psum | solution.py:84
  489.9 284.1 %all-reduce.3.cloned.1.call-start = ((), (), s32[]{:S(2)}) async-start(), calls=%async_computation.4 | async-start | bytes 884736 | tf_op jit(solution)/shard_map/psum | solution.py:83
  502.3 46.7 %copy-start.2 = (f32[16,16,8,3,128]{4,1,3,2,0:T(8,128)S(1)}, f32[16,16,8,3,128]{4,1,3,2,0:T(8,128)}, u32[]{:S(2)}) copy-start(f32[16,16,8,3,128]{4,1,3,2,0:T(8,128)} %copy.139) | copy-start | bytes 9437188
  548.9 278.3 %reduce-scatter.4.cloned.1.call-start = ((), (), s32[]{:S(2)}) async-start(), calls=%async_computation.6 | async-start | bytes 2359296
  625.2 206.2 %copy-start.1 = (bf16[3,3,3,32,64]{4,3,2,1,0:T(8,128)(2,1)S(1)}, bf16[3,3,3,32,64]{4,3,2,1,0:T(8,128)(2,1)}, u32[]{:S(2)}) copy-start(bf16[3,3,3,32,64]{4,3,2,1,0:T(8,128)(2,1)} %param.5) | copy-start | bytes 331780
Sparse Core Ops, SparseCore 0:
  206.0 170.6 all-gather.1
  490.1 135.0 all-reduce.4
  631.2 142.7 all-reduce.2
  776.3 50.8 reduce-scatter.3
where the time goes:
time: 853 us; the launch traced here: 838 us
  waiting for transfers between devices  343 us (40%)
  local copies, waits for them, and re-layouts  263 us (31%)
  matrix products  137 us (16%)
  other arithmetic  66 us (8%)
  starting transfers between devices  15.2 us (2%)
  between operations  14.4 us (2%)
    psum x1, waiting for transfers between devices, shards(): total_a = lax.psum(local_a, ('mp', 'dp'))  147 us
    transpose x2, matrix products, kernel_grad(): return jnp.transpose(result, (1, 2, 3, 0, 4))  98.3 us
    all_gather x1, waiting for transfers between devices, shards(): upstream = lax.all_gather(cotangent, 'mp', axis=4, tiled=True)  97.7 us
    unnamed x32, local copies, waits for them, and re-layouts  66.3 us
    concatenate x1, other arithmetic, shards(): padded_x = pad_sides(jnp.concatenate([below, field], axis=1))  58.2 us
    unnamed x5, waiting for transfers between devices  51.4 us
    psum x1, waiting for transfers between devices, shards(): total_b = lax.psum(local_b, 'dp')  45.1 us
    concatenate x2, local copies, waits for them, and re-layouts, shards(): padded_x = pad_sides(jnp.concatenate([below, field], axis=1))  39.5 us
  transfers between devices with their start and end apart: 7, of which 5 were waited for; matrix products, arithmetic and copies ran while one was open for 32% of the time, Pallas kernels for 0%

commit v1 on v0

--- a/solution.py
+++ b/solution.py
@@ -74,7 +74,9 @@
     features = lax.psum_scatter(partial_out, "mp", scatter_dimension=4, tiled=True).astype(
         jnp.bfloat16
     )
-    upstream = lax.all_gather(cotangent, "mp", axis=4, tiled=True)
+    upstream = jnp.concatenate(
+        lax.all_to_all(jnp.stack([cotangent] * lax.axis_size("mp")), "mp", 0, 0), axis=4
+    )
     local_b = kernel_grad(padded_h, upstream)
     back_group = input_grad(upstream, kernel_b, 1).astype(jnp.bfloat16)
     back = lax.all_to_all(back_group, "mp", split_axis=1, concat_axis=4, tiled=True)

time: 853 us -> 796 us (0.933)
  waiting for transfers between devices: 343 us -> 212 us
  local copies, waits for them, and re-layouts: 263 us -> 331 us
    all_gather x1 -> x0, waiting for transfers between devices: 97.7 us -> none  [shards(): upstream = lax.all_gather(cotangent, 'mp', axis=4, tiled=True)]
    reshape x0 -> x5, local copies, waits for them, and re-layouts: none -> 57 us  [shards(): jnp.concatenate(lax.all_to_all(jnp.stack([cotangent] * lax.axis_size('mp'...]
    unnamed x5 -> x4, waiting for transfers between devices: 51.4 us -> 0.05 us
    unnamed x32 -> x34, local copies, waits for them, and re-layouts: 66.3 us -> 94.3 us
    all_gather x3 -> x0, local copies, waits for them, and re-layouts: 23.8 us -> none  [shards(): upstream = lax.all_gather(cotangent, 'mp', axis=4, tiled=True)]
    psum x1, waiting for transfers between devices: 45.1 us -> 56.5 us  [shards(): total_b = lax.psum(local_b, 'dp')]
  transfers between devices with their start and end apart: 7 -> 7, of which waited for: 5 -> 2; matrix products, arithmetic and copies ran while one was open for 32% -> 34% of each run, Pallas kernels for 0% -> 0%
where the time goes in v1:
time: 796 us; the launch traced here: 782 us
  local copies, waits for them, and re-layouts  331 us (42%)
  waiting for transfers between devices  212 us (27%)
  matrix products  137 us (17%)
  other arithmetic  66 us (8%)
  starting transfers between devices  20.3 us (3%)
  between operations  16.2 us (2%)
    psum x1, waiting for transfers between devices, shards(): total_a = lax.psum(local_a, ('mp', 'dp'))  155 us
    transpose x2, matrix products, kernel_grad(): return jnp.transpose(result, (1, 2, 3, 0, 4))  98.1 us
    unnamed x34, local copies, waits for them, and re-layouts  94.3 us
    concatenate x1, other arithmetic, shards(): padded_x = pad_sides(jnp.concatenate([below, field], axis=1))  58.2 us
    reshape x5, local copies, waits for them, and re-layouts, shards(): jnp.concatenate(lax.all_to_all(jnp.stack([cotangent] * lax.axis_size('mp'...  57 us
    psum x1, waiting for transfers between devices, shards(): total_b = lax.psum(local_b, 'dp')  56.5 us
    concatenate x2, local copies, waits for them, and re-layouts, shards(): padded_x = pad_sides(jnp.concatenate([below, field], axis=1))  39.5 us
    conv_general_dilated x6, local copies, waits for them, and re-layouts, forward_conv(): lax.conv_general_dilated(padded, kernel, (2, 2, 2), 'VALID', dimension_nu...  38 us
  transfers between devices with their start and end apart: 7, of which 2 were waited for; matrix products, arithmetic and copies ran while one was open for 34% of the time, Pallas kernels for 0%

profile of v1, /device:TPU:1, one launch (start us, length us, event | category | flops | bytes accessed | tf_op | source)
XLA Modules:
  0.0 781.6 jit_solution(16233525691400242126)
XLA Ops:
  8.0 4.9 copy.121
  12.9 1.1 slice.11
  13.9 1.1 copy.122
  15.0 4.0 collective-permute-start
  19.0 31.5 %copy.124 = bf16[1,8,64,64,32]{4,0,3,2,1:T(2,128)(2,1)} copy(bf16[1,8,64,64,32]{2,4,3,1,0:T(8,128)(2,1)} %bitcast.78) | data formatting | bytes 4194304 | tf_op jit(solution)/shard_map/reshape | solution.py:66
  50.6 2.7 copy.123
  53.2 58.2 %pad_maximum_fusion = bf16[1,9,64,64,32]{4,0,3,2,1:T(2,128)(2,1)} fusion(bf16[1,8,64,64,32]{4,0,3,2,1:T(2,128)(2,1)} %copy.124, bf16[1,1,64,64,32]{4,0,3,2,1:T(2,128)(2,1)S(1)} %copy.123), kind=kLoop, calls=%fused_computation.4 | loop fusion | flops 1179648 | bytes 4718592 | tf_op jit(solution)/shard_map/concatenate | solution.py:68
  111.5 33.5 %copy.125 = bf16[1,9,64,64,32]{3,4,2,1,0:T(8,128)(2,1)} copy(bf16[1,9,64,64,32]{4,0,3,2,1:T(2,128)(2,1)} %pad_maximum_fusion) | data formatting | bytes 4718592 | tf_op jit(solution)/shard_map/concatenate | solution.py:68
  144.9 9.2 %copy.155 = bf16[9,64,1,64,32]{1,4,3,0,2:T(8,128)(2,1)} copy(bf16[9,64,1,64,32]{3,4,2,1,0:T(8,128)(2,1)} %bitcast.81) | data formatting | bytes 4718592
  154.2 6.1 pad.4.clone
  160.2 15.6 %copy.128 = bf16[9,64,1,8,10,32]{5,3,4,1,0,2:T(8,128)(2,1)} copy(bf16[9,64,1,8,10,32]{1,5,4,3,0,2:T(8,128)(2,1)} %bitcast.76) | data formatting | bytes 5898240 | tf_op jit(solution)/shard_map/conv_general_dilated | solution.py:17
  175.9 2.3 slice.12
  178.2 12.0 %compare_select_fusion = (f32[4,32,8,5,64]{4,2,3,1,0:T(8,128)}, bf16[4,32,8,5,64]{4,2,3,1,0:T(8,128)(2,1)S(1)}) fusion(pred[8,5]{0,1:T(8,128)(4,1)S(1)} %copy-done.7, bf16[3,3,3,32,64]{4,3,2,1,0:T(8,128)(2,1)S(1)} %copy-done, bf16[9,64,1,7,2,32]{5,3,4,1,0,2:T(8,128)(2,1)S(1)} %slice.12, bf16[9,64,1,8,10,32]{5,3,4,1,0,2:T(8,128)(2,1)} %copy.128), kind=kOutput, calls=%fused_computation.20 | convolution fusion | flops 572915712 | bytes 5541928 | tf_op jit(solution)/shard_map/conv_general_dilated | solution.py:17
  190.3 0.3 copy.129
  190.7 3.2 copy.130
  193.9 12.8 %reshape.84 = bf16[8,2,16384]{2,1,0:T(2,128)(2,1)} reshape(bf16[64,1,4,32,32]{4,3,2,1,0:T(8,128)(2,1)S(1)} %bitcast.86) | data formatting | bytes 1048576
  206.7 5.9 all-to-all-start
  212.6 6.7 stack.2
  219.2 11.4 %reshape.86 = bf16[8,2,32768]{2,1,0:T(2,128)(2,1)} reshape(bf16[8,1,16,16,16,16]{5,4,3,2,1,0:T(8,128)(2,1)} %stack.2) | data formatting | bytes 2097152
  230.6 0.5 copy.144
  231.1 0.2 slice.18
  231.3 2.9 copy.154
  234.2 0.8 copy-done.4
  235.0 5.1 all-to-all-start.1
  240.1 3.1 reshape.85
  243.2 2.9 copy.131
  246.1 2.2 copy.132
  248.3 3.4 copy.156
  251.7 4.0 pad.6.clone
  255.7 12.8 %copy.135 = bf16[32,32,1,8,6,8]{5,3,4,1,0,2:T(8,128)(2,1)} copy(bf16[32,32,1,8,6,8]{1,5,4,3,0,2:T(8,128)(2,1)} %bitcast.82) | data formatting | bytes 1572864 | tf_op jit(solution)/shard_map/conv_general_dilated | solution.py:17
  268.5 3.4 slice.14
  272.0 12.3 %broadcast_select_fusion = f32[16,16,8,3,128]{4,2,3,1,0:T(8,128)S(1)} fusion(pred[8,3]{0,1:T(4,128)(4,1)S(1)} %copy-done.8, bf16[3,3,3,8,128]{4,3,2,1,0:T(8,128)(2,1)S(1)} %copy-done.6, bf16[32,32,1,7,2,8]{5,3,4,1,0,2:T(8,128)(2,1)S(1)} %slice.14, bf16[32,32,1,8,6,8]{5,3,4,1,0,2:T(8,128)(2,1)} %copy.135), kind=kOutput, calls=%fused_computation.30 | convolution fusion | flops 329662464 | bytes 4216856 | tf_op jit(solution)/shard_map/conv_general_dilated | solution.py:17
  284.3 2.2 copy.136
  286.5 23.8 %copy.149 = bf16[1,32,32,32,8]{4,0,3,2,1:T(2,128)(2,1)} copy(bf16[1,32,32,32,8]{3,4,2,1,0:T(8,128)(2,1)S(1)} %bitcast.80) | data formatting | bytes 1048576 | tf_op jit(solution)/shard_map/all_to_all | solution.py:71
  310.2 7.8 %reshape.87 = bf16[8,1,16,16,16,16]{5,4,3,2,1,0:T(8,128)(2,1)} reshape(bf16[8,2,32768]{2,1,0:T(2,128)(2,1)S(1)} %all-to-all-done.1) | data formatting | bytes 2097152
  318.1 13.9 %copy.137 = bf16[1,16,16,16,8,16]{5,4,2,3,1,0:T(8,128)(2,1)} copy(bf16[1,16,16,16,8,16]{5,3,2,1,0,4:T(8,128)(2,1)} %bitcast.73) | data formatting | bytes 2097152 | tf_op jit(solution)/shard_map/reshape | solution.py:77
  331.9 20.2 %copy.148 = bf16[1,16,16,16,8,16]{5,4,3,2,1,0:T(8,128)(2,1)} copy(bf16[1,16,16,16,8,16]{5,3,2,1,0,4:T(8,128)(2,1)} %bitcast.74) | data formatting | bytes 2097152 | tf_op jit(solution)/shard_map/reshape | solution.py:77
  352.2 9.3 %reshape.71 = bf16[16,16,1,16,128]{4,1,3,0,2:T(8,128)(2,1)S(1)} reshape(bf16[1,16,16,16,8,16]{5,4,2,3,1,0:T(8,128)(2,1)} %copy.137) | data formatting | bytes 2097152 | tf_op jit(solution)/shard_map/reshape | solution.py:77
  361.4 13.3 %reshape.83 = bf16[1,16,16,16,128]{4,0,3,2,1:T(2,128)(2,1)} reshape(bf16[1,16,16,16,8,16]{5,4,3,2,1,0:T(8,128)(2,1)} %copy.148) | data formatting | bytes 2097152 | tf_op jit(solution)/shard_map/reshape | solution.py:77
  374.8 0.3 pad.8
  375.1 0.4 copy.139
  375.5 0.2 slice.16
  375.7 14.3 %fusion.17 = bf16[32,32,8,6,8]{4,2,3,1,0:T(8,128)(2,1)} fusion(bf16[3,3,3,8,128]{4,3,2,1,0:T(8,128)(2,1)S(1)} %copy-done.6, bf16[16,16,1,7,1,128]{5,3,4,1,0,2:T(8,128)(2,1)S(1)} %slice.16, bf16[16,16,1,8,3,128]{5,3,4,1,0,2:T(8,128)(2,1)S(1)} %copy.139), kind=kOutput, calls=%fused_computation.24 | convolution fusion | flops 332021760 | bytes 2873344 | tf_op jit(solution)/shard_map/conv_general_dilated | solution.py:42
  390.0 13.6 %copy.140 = bf16[32,32,8,6,8]{1,4,3,2,0:T(8,128)(2,1)S(1)} copy(bf16[32,32,8,6,8]{4,2,3,1,0:T(8,128)(2,1)} %fusion.17) | data formatting | bytes 1572864 | tf_op jit(solution)/shard_map/conv_general_dilated | solution.py:42
  403.6 0.9 select_convert_fusion
  404.5 0.2 fusion.34
  404.7 2.7 reshape.88
  407.5 5.1 all-to-all-start.2
  412.6 51.5 %fusion.36 = f32[3,3,3,8,128]{4,3,2,1,0:T(8,128)} fusion(bf16[1,32,32,32,8]{4,0,3,2,1:T(2,128)(2,1)} %copy.149, bf16[1,16,16,16,128]{4,0,3,2,1:T(2,128)(2,1)} %reshape.83), kind=kOutput, calls=%fused_computation.46 | convolution fusion | flops 212629504 | bytes 1683456 | tf_op jit(solution)/shard_map/transpose | solution.py:37
  464.2 1.3 reshape.89
  465.5 3.4 copy.142
  469.0 3.5 fusion.12
  472.5 4.1 copy.146
  476.6 46.6 %fusion.35 = f32[3,3,3,32,64]{4,3,2,1,0:T(8,128)} fusion(bf16[1,9,64,64,32]{4,0,3,2,1:T(2,128)(2,1)} %pad_maximum_fusion, bf16[1,4,32,32,64]{4,0,3,2,1:T(2,128)(2,1)} %copy.146), kind=kOutput, calls=%fused_computation.45 | convolution fusion | flops 443596800 | bytes 3104768 | tf_op jit(solution)/shard_map/transpose | solution.py:37
  523.2 1.6 slice_bitcast_fusion.1
  524.8 14.3 %copy.152 = f32[1,16,16,16,128]{2,3,1,0,4:T(8,128)} copy(f32[1,16,16,16,128]{4,2,3,1,0:T(8,128)} %slice_bitcast_fusion.1) | data formatting | bytes 4194304
  539.1 15.3 %reshape.81 = f32[128,4096]{1,0:T(8,128)} reshape(f32[128,1,16,16,16]{4,3,2,1,0:T(8,128)} %bitcast.75) | data formatting | bytes 4194304
  554.4 56.5 %all-reduce.5.cloned.1.call-done = f32[3,3,3,8,128]{4,3,2,1,0:T(8,128)} async-done(((f32[3,3,3,8,128]{4,3,2,1,0:T(8,128)}), f32[3,3,3,8,128]{4,3,2,1,0:T(8,128)}) %all-reduce.5.cloned.1.call-update) | async-done | bytes 110608 | tf_op jit(solution)/shard_map/psum | solution.py:86
  610.9 1.5 broadcast_multiply_fusion.1
  612.5 155.2 %all-reduce.3.cloned.1.call-done = f32[3,3,3,32,64]{4,3,2,1,0:T(8,128)} async-done(((f32[3,3,3,32,64]{4,3,2,1,0:T(8,128)}), f32[3,3,3,32,64]{4,3,2,1,0:T(8,128)}) %all-reduce.3.cloned.1.call-update) | async-done | bytes 221200 | tf_op jit(solution)/shard_map/psum | solution.py:85
  767.7 1.8 broadcast_multiply_fusion
  769.5 1.7 reshape.82
  771.3 1.2 copy.153
  772.5 1.2 copy.151
  (29 shorter events, 0.3 us)
Async XLA Ops:
  8.0 170.2 %copy-start = (bf16[3,3,3,32,64]{4,3,2,1,0:T(8,128)(2,1)S(1)}, bf16[3,3,3,32,64]{4,3,2,1,0:T(8,128)(2,1)}, u32[]{:S(2)}) copy-start(bf16[3,3,3,32,64]{4,3,2,1,0:T(8,128)(2,1)} %param.5) | copy-start | bytes 331780
  15.0 35.5 %collective-permute-start = (bf16[1,1,64,64,32]{3,4,2,1,0:T(8,128)(2,1)S(1)}, bf16[1,1,64,64,32]{3,4,2,1,0:T(8,128)(2,1)S(1)}, u32[]{:S(2)}, u32[]{:S(2)}) collective-permute-start(bf16[1,1,64,64,32]{3,4,2,1,0:T(8,128)(2,1)S(1)} %copy.122), channel_id=1, source_target_pairs={{0,16},{16,32},{32,48},{48,64},{64,80},{80,96},{96,112},{1,17},{17... | collective-permute-start | bytes 786440 | tf_op jit(solution)/shard_map/ppermute | solution.py:13
  175.9 2.4 copy-start.7
  206.7 27.5 %all-to-all-start = ((bf16[8,2,16384]{2,1,0:T(2,128)(2,1)}), bf16[8,2,16384]{2,1,0:T(2,128)(2,1)S(1)}, u32[]{:S(2)}, u32[]{:S(2)}) async-start(bf16[8,2,16384]{2,1,0:T(2,128)(2,1)} %reshape.84), calls=%async_computation | async-start | bytes 1048576 | tf_op jit(solution)/shard_map/all_to_all | solution.py:71
  219.2 11.4 %copy-start.3 = (f32[4,32,8,5,64]{4,2,3,1,0:T(8,128)S(1)}, f32[4,32,8,5,64]{4,2,3,1,0:T(8,128)}, u32[]{:S(2)}) copy-start(f32[4,32,8,5,64]{4,2,3,1,0:T(8,128)} %get-tuple-element.18) | copy-start | bytes 3932164
  234.2 0.8 copy-start.4
  235.0 75.2 %all-to-all-start.1 = ((bf16[8,2,32768]{2,1,0:T(2,128)(2,1)}), bf16[8,2,32768]{2,1,0:T(2,128)(2,1)S(1)}, u32[]{:S(2)}, u32[]{:S(2)}) async-start(bf16[8,2,32768]{2,1,0:T(2,128)(2,1)} %reshape.86), calls=%async_computation.1 | async-start | bytes 2097152 | tf_op jit(solution)/shard_map/all_to_all | solution.py:78
  268.5 3.4 copy-start.6
  268.5 3.4 copy-start.8
  390.0 13.6 %copy-start.5 = (pred[8,6]{1,0:T(8,128)(4,1)S(1)}, pred[8,6]{1,0:T(8,128)(4,1)}, u32[]{:S(2)}) copy-start(pred[8,6]{1,0:T(8,128)(4,1)} %constant.31) | copy-start | bytes 148
  407.5 56.8 %all-to-all-start.2 = ((bf16[8,2,16384]{2,1,0:T(2,128)(2,1)}), bf16[8,2,16384]{2,1,0:T(2,128)(2,1)S(1)}, u32[]{:S(2)}, u32[]{:S(2)}) async-start(bf16[8,2,16384]{2,1,0:T(2,128)(2,1)} %reshape.88), calls=%async_computation.2 | async-start | bytes 1048576 | tf_op jit(solution)/shard_map/all_to_all | solution.py:82
  412.6 198.3 %all-reduce.5.cloned.1.call-start = ((), (), s32[]{:S(2)}) async-start(), calls=%async_computation.5 | async-start | bytes 221184 | tf_op jit(solution)/shard_map/psum | solution.py:86
  464.2 303.5 %all-reduce.3.cloned.1.call-start = ((), (), s32[]{:S(2)}) async-start(), calls=%async_computation.4 | async-start | bytes 884736 | tf_op jit(solution)/shard_map/psum | solution.py:85
  476.5 46.7 %copy-start.2 = (f32[16,16,8,3,128]{4,1,3,2,0:T(8,128)S(1)}, f32[16,16,8,3,128]{4,1,3,2,0:T(8,128)}, u32[]{:S(2)}) copy-start(f32[16,16,8,3,128]{4,1,3,2,0:T(8,128)} %copy.136) | copy-start | bytes 9437188
  523.2 246.4 %reduce-scatter.4.cloned.1.call-start = ((), (), s32[]{:S(2)}) async-start(), calls=%async_computation.6 | async-start | bytes 2359296
  554.3 219.4 %copy-start.1 = (bf16[3,3,3,32,64]{4,3,2,1,0:T(8,128)(2,1)S(1)}, bf16[3,3,3,32,64]{4,3,2,1,0:T(8,128)(2,1)}, u32[]{:S(2)}) copy-start(bf16[3,3,3,32,64]{4,3,2,1,0:T(8,128)(2,1)} %param.5) | copy-start | bytes 331780
Sparse Core Ops, SparseCore 0:
  464.3 146.5 all-reduce.4
  617.0 150.6 all-reduce.2
Sparse Core Ops, SparseCore 1:
  554.5 55.8 reduce-scatter.3
